TPU v7x, 32 devices: a whole 2x2x4 slice. The times are simulated.
32 devices in a mesh: grp: 2 (over y), tile: 8 (over z, x), chan: 2 (over core).
Axes of the slice: x: 2, y: 2, z: 4, core: 2. Of those that a mesh axis runs over, the one named last changes fastest.
Arguments:
- sketch_vectors: bfloat16 [8, 16, 256, 256], P(None, 'tile', 'grp', 'chan'), parts along dimension 2, may hold values from -6 to 6
- base_state: bfloat16 [8, 32, 256], P(None, ('grp', 'tile'), 'chan'), parts along dimension 1, may hold values from -6 to 6
- depth_taps: bfloat16 [3, 9, 256], P(None, None, 'chan'), may hold values from -2 to 2
- mix_weight: bfloat16 [3, 256, 256], P(None, None, 'chan'), may hold values from -0.375 to 0.375
Outputs:
- images: bfloat16 [8, 16, 256, 256], P(None, 'tile', 'grp', 'chan'), parts along dimension 2
- gram: float32 [4, 128, 128], P('grp'), parts along dimension 0
There are 2 independent parts, one for each index of `grp`. A program takes and returns all parts, laid end to end along the dimension named above; an argument that names none is the same for every part. Nothing has to cross between parts.
All inputs are finite; a program needn't handle non-finite values.
Results may differ from a plain program's by a relative error of at most 0.002.
The roundings to bfloat16 on the way count: a program that leaves them out, or rounds other values in their place, can miss the bound.
Values may be sent and summed in bfloat16 or wider, within the bound.
A program may use at most 64 MiB of HBM per device.

v0:
```python
import jax
import jax.numpy as jnp
from jax import lax
from jax.sharding import PartitionSpec as P

LAYERS = 3


def extended_2(block, sides, width):
    for axis, dim in sides:
        count = lax.axis_size(axis)
        forward = [(i, i + 1) for i in range(count - 1)]
        forward.append((count - 1, 0))
        backward = [(target, source) for source, target in forward]
        low = lax.ppermute(
            lax.slice_in_dim(block, block.shape[dim] - width, None, axis=dim), axis, forward
        )
        high = lax.ppermute(lax.slice_in_dim(block, 0, width, axis=dim), axis, backward)
        block = jnp.concatenate([low, block, high], axis=dim)
    return block


def convolve(extended, tap_rows, width):
    height = extended.shape[0]
    padded = jnp.pad(extended, ((2, 2), (0, 0), (0, 0), (0, 0)))
    summed = jnp.zeros((height, width) + extended.shape[2:], jnp.float32)
    for row_tap in range(3):
        for col_tap in range(3):
            weight_row = tap_rows[3 * row_tap + col_tap].astype(jnp.float32)
            window = padded[2 * row_tap : 2 * row_tap + height, 2 * col_tap : 2 * col_tap + width]
            summed = summed + weight_row * window.astype(jnp.float32)
    return summed.astype(jnp.bfloat16)


def advance(fields, mixed):
    slope = jnp.tanh(mixed[:, :, 0:1, :])
    base_next = fields[:, :, 0:1, :].astype(jnp.float32) + slope
    vec_next = fields[:, :, 1:, :].astype(jnp.float32) + (1.0 - slope * slope) * mixed[:, :, 1:, :]
    return jnp.concatenate([base_next, vec_next], axis=2).astype(jnp.bfloat16)


def per_device(sketch_vectors, base_state, depth_taps, mix_weight):
    width = sketch_vectors.shape[1]
    fields = jnp.concatenate([base_state[:, :, None, :], sketch_vectors], axis=2)
    for layer in range(LAYERS):
        extended = extended_2(fields, (("tile", 1),), 2)
        conv = convolve(extended, depth_taps[layer], width)
        layer_mix = mix_weight[layer]
        mixed = jnp.dot(
            lax.all_gather(conv, "chan", axis=3, tiled=True),
            layer_mix,
            preferred_element_type=jnp.float32,
        )
        fields = advance(fields, mixed)
    images = fields[:, :, 1:, :]
    num_vectors = images.shape[2]
    flat_images = images.reshape(-1, num_vectors, images.shape[3])
    flat_sketch = sketch_vectors.reshape(-1, num_vectors, images.shape[3])
    first = jnp.einsum("pkc,pjc->kj", flat_images, flat_images, preferred_element_type=jnp.float32)
    second = jnp.einsum("pkc,pjc->kj", flat_sketch, flat_images, preferred_element_type=jnp.float32)
    total_cells = (
        images.shape[0] * width * lax.axis_size("tile") * images.shape[3] * lax.axis_size("chan")
    )
    summed = lax.psum(jnp.stack([first, second]), ("tile", "chan"))
    return (images, summed / total_cells)


def solution(mesh):
    in_specs = (
        P(None, "tile", "grp", "chan"),
        P(None, ("grp", "tile"), "chan"),
        P(None, None, "chan"),
        P(None, None, "chan"),
    )
    out_specs = (P(None, "tile", "grp", "chan"), P("grp", None, None))
    return jax.shard_map(
        per_device, mesh=mesh, in_specs=in_specs, out_specs=out_specs, check_vma=False
    )
```

profile of v0, /device:TPU:0, one launch (start us, length us, event | category | flops | bytes accessed | tf_op | source)
XLA Modules:
  0.0 234.1 jit_solution(14303689334135665172)
XLA Ops:
  7.2 0.0 copy-start.3
  7.2 0.0 all-gather.4.cloned.1.call-start
  7.2 0.7 copy.96
  7.9 1.2 pad_maximum_fusion
  9.1 0.1 copy.35
  9.3 0.0 copy-start
  9.3 3.0 %collective-permute-start = (bf16[8,2,129,128]{3,0,2,1:T(8,128)(2,1)S(1)}, bf16[8,2,129,128]{3,0,2,1:T(8,128)(2,1)S(1)}, u32[]{:S(2)}, u32[]{:S(2)}) collective-permute-start(bf16[8,2,129,128]{3,0,2,1:T(8,128)(2,1)S(1)} %copy.35), channel_id=1, source_target_pairs={{0,2},{2,4},{4,6},{6,8},{8,10},{10,12},{12,14},{14,0},{1,3},{3,5},... | collective-permute-start | bytes 1585160 | tf_op jit(solution)/shard_map/ppermute | solution.py:15
  12.3 3.1 %collective-permute-start.1 = (bf16[8,2,129,128]{3,0,2,1:T(8,128)(2,1)S(1)}, bf16[8,2,129,128]{3,0,2,1:T(8,128)(2,1)S(1)}, u32[]{:S(2)}, u32[]{:S(2)}) collective-permute-start(bf16[8,2,129,128]{3,0,2,1:T(8,128)(2,1)S(1)} %copy.35), channel_id=1, source_target_pairs={{2,0},{4,2},{6,4},{8,6},{10,8},{12,10},{14,12},{0,14},{3,1},{5,3},... | collective-permute-start | bytes 1585160 | tf_op jit(solution)/shard_map/ppermute | solution.py:18
  15.4 0.0 copy-done.3
  15.4 19.5 %collective-permute-done = bf16[8,2,129,128]{3,0,2,1:T(8,128)(2,1)S(1)} collective-permute-done((bf16[8,2,129,128]{3,0,2,1:T(8,128)(2,1)S(1)}, bf16[8,2,129,128]{3,0,2,1:T(8,128)(2,1)S(1)}, u32[]{:S(2)}, u32[]{:S(2)}) %collective-permute-start) | collective-permute-done | bytes 528416 | tf_op jit(solution)/shard_map/ppermute | solution.py:15
  34.9 0.1 copy.37
  34.9 2.1 collective-permute-done.1
  37.1 0.1 copy.38
  37.1 0.0 copy-done
  37.2 1.6 select_maximum_fusion.6
  38.8 0.0 copy-start.2
  38.8 1.9 add_convert_fusion.2
  40.7 0.0 all-gather.4.cloned.1.call-update
  40.7 0.0 copy-start.4
  40.7 0.0 all-gather.6.cloned.1.call-start
  40.7 9.3 %all-gather.4.cloned.1.call-done = bf16[8,2,129,256]{3,2,1,0:T(8,128)(2,1)} async-done(((bf16[8,2,129,128]{3,2,1,0:T(8,128)(2,1)}), bf16[8,2,129,256]{3,2,1,0:T(8,128)(2,1)}) %all-gather.4.cloned.1.call-update) | async-done | bytes 1056784 | tf_op jit(solution)/shard_map/all_gather | solution.py:50
  50.0 0.0 copy-done.2
  50.0 1.7 fusion.14
  51.7 0.0 copy-done.4
  51.8 0.2 fusion.9
  52.0 0.2 pad_maximum_fusion.1
  52.2 0.1 copy.44
  52.3 1.8 collective-permute-start.2
  54.1 3.0 %collective-permute-start.3 = (bf16[8,2,129,128]{3,0,2,1:T(8,128)(2,1)S(1)}, bf16[8,2,129,128]{3,0,2,1:T(8,128)(2,1)S(1)}, u32[]{:S(2)}, u32[]{:S(2)}) collective-permute-start(bf16[8,2,129,128]{3,0,2,1:T(8,128)(2,1)S(1)} %copy.44), channel_id=1, source_target_pairs={{2,0},{4,2},{6,4},{8,6},{10,8},{12,10},{14,12},{0,14},{3,1},{5,3},... | collective-permute-start | bytes 1585160 | tf_op jit(solution)/shard_map/ppermute | solution.py:18
  57.1 20.1 %collective-permute-done.2 = bf16[8,2,129,128]{3,0,2,1:T(8,128)(2,1)S(1)} collective-permute-done((bf16[8,2,129,128]{3,0,2,1:T(8,128)(2,1)S(1)}, bf16[8,2,129,128]{3,0,2,1:T(8,128)(2,1)S(1)}, u32[]{:S(2)}, u32[]{:S(2)}) %collective-permute-start.2) | collective-permute-done | bytes 528416 | tf_op jit(solution)/shard_map/ppermute | solution.py:15
  77.2 0.1 copy.46
  77.2 2.1 collective-permute-done.3
  79.4 0.1 copy.47
  79.4 1.6 select_maximum_fusion.3
  81.1 1.9 add_convert_fusion.1
  82.9 0.0 all-gather.6.cloned.1.call-update
  82.9 0.0 all-gather.8.cloned.1.call-start
  83.0 9.0 %all-gather.6.cloned.1.call-done = bf16[8,2,129,256]{3,2,1,0:T(8,128)(2,1)} async-done(((bf16[8,2,129,128]{3,2,1,0:T(8,128)(2,1)}), bf16[8,2,129,256]{3,2,1,0:T(8,128)(2,1)}) %all-gather.6.cloned.1.call-update) | async-done | bytes 1056784 | tf_op jit(solution)/shard_map/all_gather | solution.py:50
  92.0 1.7 fusion.12
  93.7 0.2 fusion.7
  94.0 0.2 pad_maximum_fusion.2
  94.1 0.1 copy.53
  94.3 1.8 collective-permute-start.4
  96.1 3.0 %collective-permute-start.5 = (bf16[8,2,129,128]{3,0,2,1:T(8,128)(2,1)S(1)}, bf16[8,2,129,128]{3,0,2,1:T(8,128)(2,1)S(1)}, u32[]{:S(2)}, u32[]{:S(2)}) collective-permute-start(bf16[8,2,129,128]{3,0,2,1:T(8,128)(2,1)S(1)} %copy.53), channel_id=1, source_target_pairs={{2,0},{4,2},{6,4},{8,6},{10,8},{12,10},{14,12},{0,14},{3,1},{5,3},... | collective-permute-start | bytes 1585160 | tf_op jit(solution)/shard_map/ppermute | solution.py:18
  99.0 20.1 %collective-permute-done.4 = bf16[8,2,129,128]{3,0,2,1:T(8,128)(2,1)S(1)} collective-permute-done((bf16[8,2,129,128]{3,0,2,1:T(8,128)(2,1)S(1)}, bf16[8,2,129,128]{3,0,2,1:T(8,128)(2,1)S(1)}, u32[]{:S(2)}, u32[]{:S(2)}) %collective-permute-start.4) | collective-permute-done | bytes 528416 | tf_op jit(solution)/shard_map/ppermute | solution.py:15
  119.1 0.1 copy.55
  119.2 2.1 collective-permute-done.5
  121.3 0.1 copy.56
  121.4 1.6 select_maximum_fusion
  123.0 1.9 add_convert_fusion
  124.9 0.0 all-gather.8.cloned.1.call-update
  124.9 0.0 all-reduce.5.cloned.1.call-start
  124.9 9.0 %all-gather.8.cloned.1.call-done = bf16[8,2,129,256]{3,2,1,0:T(8,128)(2,1)} async-done(((bf16[8,2,129,128]{3,2,1,0:T(8,128)(2,1)}), bf16[8,2,129,256]{3,2,1,0:T(8,128)(2,1)}) %all-gather.8.cloned.1.call-update) | async-done | bytes 1056784 | tf_op jit(solution)/shard_map/all_gather | solution.py:50
  133.9 1.7 fusion.10
  135.7 0.2 fusion.5
  135.9 0.0 copy-start.1
  135.9 0.3 convolution_bitcast_fusion.1
  136.2 0.3 convolution_bitcast_fusion
  136.5 0.2 copy-done.1
  136.7 0.7 pad_maximum_fusion.3
  137.3 0.0 all-reduce.5.cloned.1.call-update
  137.4 88.6 %all-reduce.5.cloned.1.call-done = f32[2,128,128]{2,1,0:T(8,128)} async-done(((f32[2,128,128]{2,1,0:T(8,128)}), f32[2,128,128]{2,1,0:T(8,128)}) %all-reduce.5.cloned.1.call-update) | async-done | bytes 131088 | tf_op jit(solution)/shard_map/psum | solution.py:64
  226.0 1.6 broadcast_multiply_fusion
  (14 shorter events, 0.1 us)
Async XLA Ops:
  7.2 8.2 %copy-start.3 = (bf16[3,9,128]{2,0,1:T(4,128)(2,1)S(1)}, bf16[3,9,128]{2,0,1:T(4,128)(2,1)}, u32[]{:S(2)}) copy-start(bf16[3,9,128]{2,0,1:T(4,128)(2,1)} %param.6) | copy-start | bytes 20740
  7.2 42.9 %all-gather.4.cloned.1.call-start = ((), (), s32[]{:S(2)}) async-start(), calls=%async_computation | async-start | bytes 1671168 | tf_op jit(solution)/shard_map/all_gather | solution.py:50
  9.3 27.9 %copy-start = (bf16[8,2,128,128]{3,2,1,0:T(8,128)(2,1)S(1)}, bf16[8,2,128,128]{3,2,1,0:T(8,128)(2,1)}, u32[]{:S(2)}) copy-start(bf16[8,2,128,128]{3,2,1,0:T(8,128)(2,1)} %param.4) | copy-start | bytes 1572868
  9.3 25.6 %collective-permute-start = (bf16[8,2,129,128]{3,0,2,1:T(8,128)(2,1)S(1)}, bf16[8,2,129,128]{3,0,2,1:T(8,128)(2,1)S(1)}, u32[]{:S(2)}, u32[]{:S(2)}) collective-permute-start(bf16[8,2,129,128]{3,0,2,1:T(8,128)(2,1)S(1)} %copy.35), channel_id=1, source_target_pairs={{0,2},{2,4},{4,6},{6,8},{8,10},{10,12},{12,14},{14,0},{1,3},{3,5},... | collective-permute-start | bytes 1585160 | tf_op jit(solution)/shard_map/ppermute | solution.py:15
  12.3 24.8 %collective-permute-start.1 = (bf16[8,2,129,128]{3,0,2,1:T(8,128)(2,1)S(1)}, bf16[8,2,129,128]{3,0,2,1:T(8,128)(2,1)S(1)}, u32[]{:S(2)}, u32[]{:S(2)}) collective-permute-start(bf16[8,2,129,128]{3,0,2,1:T(8,128)(2,1)S(1)} %copy.35), channel_id=1, source_target_pairs={{2,0},{4,2},{6,4},{8,6},{10,8},{12,10},{14,12},{0,14},{3,1},{5,3},... | collective-permute-start | bytes 1585160 | tf_op jit(solution)/shard_map/ppermute | solution.py:18
  38.8 11.3 %copy-start.2 = (bf16[3,256,128]{2,1,0:T(8,128)(2,1)S(1)}, bf16[3,256,128]{2,1,0:T(8,128)(2,1)}, u32[]{:S(2)}) copy-start(bf16[3,256,128]{2,1,0:T(8,128)(2,1)} %param.7) | copy-start | bytes 589828
  40.7 11.1 %copy-start.4 = (bf16[8,2,128]{2,1,0:T(2,128)(2,1)S(1)}, bf16[8,2,128]{2,1,0:T(2,128)(2,1)}, u32[]{:S(2)}) copy-start(bf16[8,2,128]{2,1,0:T(2,128)(2,1)} %param.5) | copy-start | bytes 12292
  40.7 51.3 %all-gather.6.cloned.1.call-start = ((), (), s32[]{:S(2)}) async-start(), calls=%async_computation.1 | async-start | bytes 1671168 | tf_op jit(solution)/shard_map/all_gather | solution.py:50
  52.3 24.8 %collective-permute-start.2 = (bf16[8,2,129,128]{3,0,2,1:T(8,128)(2,1)S(1)}, bf16[8,2,129,128]{3,0,2,1:T(8,128)(2,1)S(1)}, u32[]{:S(2)}, u32[]{:S(2)}) collective-permute-start(bf16[8,2,129,128]{3,0,2,1:T(8,128)(2,1)S(1)} %copy.44), channel_id=1, source_target_pairs={{0,2},{2,4},{4,6},{6,8},{8,10},{10,12},{12,14},{14,0},{1,3},{3,5},... | collective-permute-start | bytes 1585160 | tf_op jit(solution)/shard_map/ppermute | solution.py:15
  54.1 25.2 %collective-permute-start.3 = (bf16[8,2,129,128]{3,0,2,1:T(8,128)(2,1)S(1)}, bf16[8,2,129,128]{3,0,2,1:T(8,128)(2,1)S(1)}, u32[]{:S(2)}, u32[]{:S(2)}) collective-permute-start(bf16[8,2,129,128]{3,0,2,1:T(8,128)(2,1)S(1)} %copy.44), channel_id=1, source_target_pairs={{2,0},{4,2},{6,4},{8,6},{10,8},{12,10},{14,12},{0,14},{3,1},{5,3},... | collective-permute-start | bytes 1585160 | tf_op jit(solution)/shard_map/ppermute | solution.py:18
  82.9 51.0 %all-gather.8.cloned.1.call-start = ((), (), s32[]{:S(2)}) async-start(), calls=%async_computation.2 | async-start | bytes 1671168 | tf_op jit(solution)/shard_map/all_gather | solution.py:50
  94.3 24.8 %collective-permute-start.4 = (bf16[8,2,129,128]{3,0,2,1:T(8,128)(2,1)S(1)}, bf16[8,2,129,128]{3,0,2,1:T(8,128)(2,1)S(1)}, u32[]{:S(2)}, u32[]{:S(2)}) collective-permute-start(bf16[8,2,129,128]{3,0,2,1:T(8,128)(2,1)S(1)} %copy.53), channel_id=1, source_target_pairs={{0,2},{2,4},{4,6},{6,8},{8,10},{10,12},{12,14},{14,0},{1,3},{3,5},... | collective-permute-start | bytes 1585160 | tf_op jit(solution)/shard_map/ppermute | solution.py:15
  96.1 25.2 %collective-permute-start.5 = (bf16[8,2,129,128]{3,0,2,1:T(8,128)(2,1)S(1)}, bf16[8,2,129,128]{3,0,2,1:T(8,128)(2,1)S(1)}, u32[]{:S(2)}, u32[]{:S(2)}) collective-permute-start(bf16[8,2,129,128]{3,0,2,1:T(8,128)(2,1)S(1)} %copy.53), channel_id=1, source_target_pairs={{2,0},{4,2},{6,4},{8,6},{10,8},{12,10},{14,12},{0,14},{3,1},{5,3},... | collective-permute-start | bytes 1585160 | tf_op jit(solution)/shard_map/ppermute | solution.py:18
  124.9 101.1 %all-reduce.5.cloned.1.call-start = ((), (), s32[]{:S(2)}) async-start(), calls=%async_computation.3 | async-start | bytes 262144 | tf_op jit(solution)/shard_map/psum | solution.py:64
  135.9 0.8 copy-start.1
Sparse Core Ops, SparseCore 0:
  40.8 9.1 all-gather.3
  83.1 8.8 all-gather.5
  125.0 8.8 all-gather.7
  137.8 88.1 all-reduce.4
where the time goes:
time: 235 us; the launch traced here: 234 us
  waiting for transfers between devices  182 us (77%)
  starting transfers between devices  15.8 us (7%)
  other arithmetic  14.8 us (6%)
  between operations  14.1 us (6%)
  matrix products  5.62 us (2%)
    psum x1, waiting for transfers between devices, per_device(): summed = lax.psum(jnp.stack([first, second]), ('tile', 'chan'))  88.6 us
    ppermute x3, waiting for transfers between devices, extended_2(): lax.ppermute(lax.slice_in_dim(block, block.shape[dim] - width, None, axis...  59.6 us
    all_gather x3, waiting for transfers between devices, per_device(): lax.all_gather(conv, 'chan', axis=3, tiled=True)  27.3 us
    ppermute x3, starting transfers between devices, extended_2(): lax.ppermute(lax.slice_in_dim(block, 0, width, axis=dim), axis, backward)  9.04 us
    ppermute x3, starting transfers between devices, extended_2(): lax.ppermute(lax.slice_in_dim(block, block.shape[dim] - width, None, axis...  6.61 us
    ppermute x3, waiting for transfers between devices, extended_2(): lax.ppermute(lax.slice_in_dim(block, 0, width, axis=dim), axis, backward)  6.36 us
    convert_element_type x3, other arithmetic, convolve(): return summed.astype(jnp.bfloat16)  5.58 us
    dot_general x3, matrix products, per_device(): jnp.dot(lax.all_gather(conv, 'chan', axis=3, tiled=True), layer_mix, pref...  5.04 us
  transfers between devices with their start and end apart: 10, of which 10 were waited for; matrix products, arithmetic and copies ran while one was open for 0% of the time, Pallas kernels for 0%

commit v1 on v0

--- a/solution.py
+++ b/solution.py
@@ -1,9 +1,16 @@
+import functools
+
 import jax
 import jax.numpy as jnp
 from jax import lax
+from jax.experimental import pallas as pl
+from jax.experimental.pallas import tpu as pltpu
 from jax.sharding import PartitionSpec as P
 
 LAYERS = 3
+MESH = pl.DeviceIdType.MESH
+BF16 = jnp.bfloat16
+F32 = jnp.float32
 
 
 def extended_2(block, sides, width):
@@ -65,6 +72,349 @@
     return (images, summed / total_cells)
 
 
+def transposed_kernel(
+    tiles, chans, scale, sk_hbm, base_ref, taps_ref, mix_hbm, img_hbm, gram_ref,
+    fields, sketch, img, weights, taps, base_rows, base_all, conv, gain, acc, part, total,
+    local_sem, own_sem, base_send, base_recv, pair_send, pair_recv,
+    in_send, in_recv, out_send, out_recv, red_send, red_recv, all_send, all_recv,
+):
+    group, tile, chan = lax.axis_index("grp"), lax.axis_index("tile"), lax.axis_index("chan")
+    count = tiles * chans
+    me = tile * chans + chan
+    rows, _, _, num_vectors, width = sk_hbm.shape
+    per_tile = num_vectors // tiles
+    channels = chans * width
+    share = 2 * num_vectors // count
+
+    def device(index):
+        return lax.div(index, chans), lax.rem(index, chans)
+
+    def target(step):
+        return device(lax.rem(me + step, count))
+
+    def source(step):
+        return device(lax.rem(me - step + count, count))
+
+    def lanes(c):
+        return pl.ds(pl.multiple_of(c * width, width), width)
+
+    def vectors(t):
+        return pl.ds(pl.multiple_of(t * per_tile, per_tile), per_tile)
+
+    def share_of(index):
+        return pl.ds(pl.multiple_of(index * share, share), share)
+
+    def remote(src, dst, send, recv, to):
+        return pltpu.make_async_remote_copy(
+            src_ref=src, dst_ref=dst, send_sem=send, recv_sem=recv,
+            device_id=(group, to[0], to[1]), device_id_type=MESH,
+        )
+
+    def each_step(body):
+        def wrapped(step, carry):
+            body(step)
+            return carry
+
+        lax.fori_loop(1, count, wrapped, 0)
+
+    def copy_in(parity, step, to, of):
+        return remote(
+            sk_hbm.at[:, parity, to[1], vectors(to[0]), :],
+            fields.at[parity, of[0], :, :, lanes(of[1])],
+            in_send.at[parity, step], in_recv.at[parity, step], to,
+        )
+
+    def copy_out(parity, step, to, of):
+        return remote(
+            fields.at[parity, to[0], :, :, lanes(to[1])],
+            img.at[parity, of[1], :, vectors(of[0]), :],
+            out_send.at[parity, step], out_recv.at[parity, step], to,
+        )
+
+    def copy_base(step, to, of):
+        return remote(
+            base_all.at[tile, chan], base_all.at[of[0], of[1]],
+            base_send.at[step], base_recv.at[step], to,
+        )
+
+    def copy_part(step, to):
+        return remote(
+            acc.at[share_of(to[0] * chans + to[1])], part.at[step],
+            red_send.at[step], red_recv.at[step], to,
+        )
+
+    def copy_total(step, to, of):
+        return remote(
+            total.at[share_of(me)], total.at[share_of(of[0] * chans + of[1])],
+            all_send.at[step], all_recv.at[step], to,
+        )
+
+    mine = (tile, chan)
+    barrier = pltpu.get_barrier_semaphore()
+
+    def greet(step):
+        to = target(step)
+        pl.semaphore_signal(barrier, inc=1, device_id=(group, to[0], to[1]), device_id_type=MESH)
+
+    each_step(greet)
+
+    weights_here = pltpu.make_async_copy(mix_hbm, weights.at[:, :, lanes(chan)], local_sem.at[0])
+    sketch_here = pltpu.make_async_copy(sk_hbm, sketch, local_sem.at[1])
+    own_in = [
+        pltpu.make_async_copy(
+            sk_hbm.at[:, parity, chan, vectors(tile), :],
+            fields.at[parity, tile, :, :, lanes(chan)],
+            own_sem.at[0, parity],
+        )
+        for parity in range(2)
+    ]
+    weights_here.start()
+    own_in[0].start()
+    own_in[1].start()
+    sketch_here.start()
+
+    taps[:, :, lanes(chan)] = jnp.zeros((LAYERS, 16, width), F32)
+    for layer in range(LAYERS):
+        taps[layer, 0:9, lanes(chan)] = taps_ref[layer].astype(F32)
+    lat = base_ref.shape[0]
+    for row in range(lat):
+        pair = base_ref[row].astype(F32)
+        for parity in range(2):
+            base_rows[parity * lat + row : parity * lat + row + 1, :] = pair[parity : parity + 1]
+    base_all[tile, chan] = base_rows[...].astype(BF16)
+
+    pl.semaphore_wait(barrier, count - 1)
+
+    each_step(lambda step: copy_base(step, target(step), mine).start())
+    other = (tile, lax.rem(chan + 1, chans))
+
+    def copy_taps(of):
+        return remote(
+            taps.at[:, :, lanes(chan)], taps.at[:, :, lanes(of[1])],
+            pair_send.at[0], pair_recv.at[0], other,
+        )
+
+    def copy_weights(of):
+        return remote(
+            mix_hbm, weights.at[:, :, lanes(of[1])], pair_send.at[1], pair_recv.at[1], other
+        )
+
+    copy_taps(mine).start()
+    copy_weights(mine).start()
+    for parity in range(2):
+        each_step(lambda step: copy_in(parity, step, target(step), mine).start())
+
+    copy_taps(other).wait_recv()
+    copy_weights(other).wait_recv()
+    weights_here.wait()
+    each_step(lambda step: copy_base(step, target(step), source(step)).wait_recv())
+    base = []
+    for t in range(tiles):
+        halves = []
+        for c in range(chans):
+            both = base_all[t, c].astype(F32)
+            halves.append(jnp.where(chan == 0, both[:lat], both[lat:]))
+        base.append(jnp.concatenate(halves, axis=1))
+    edge = jnp.zeros((2, channels), F32)
+    for layer in range(LAYERS):
+        summed = []
+        for t in range(tiles):
+            by_row = []
+            for a in range(3):
+                row_sum = None
+                for b in range(3):
+                    tap = taps[layer, 3 * a + b : 3 * a + b + 1, :]
+                    term = tap * base[(t + b - 1) % tiles]
+                    row_sum = term if row_sum is None else row_sum + term
+                by_row.append(row_sum)
+            summed.append(
+                jnp.concatenate([edge, by_row[0][: lat - 2]], axis=0)
+                + by_row[1]
+                + jnp.concatenate([by_row[2][2:], edge], axis=0)
+            )
+        mixed = jnp.dot(
+            jnp.concatenate(summed, axis=0).astype(BF16), weights[layer],
+            preferred_element_type=F32,
+        )
+        slope = jnp.tanh(mixed)
+        gain[layer] = 1.0 - slope * slope
+        base = [
+            (base[t] + slope[t * lat : (t + 1) * lat]).astype(BF16).astype(F32)
+            for t in range(tiles)
+        ]
+
+    def run_layers(parity):
+        for layer in range(LAYERS):
+
+            def convolve_tile(t, carry):
+                near = (lax.rem(t + tiles - 1, tiles), t, lax.rem(t + 1, tiles))
+                for c in range(chans):
+                    part_lanes = slice(c * width, (c + 1) * width)
+                    cols = [fields[parity, n, :, :, part_lanes].astype(F32) for n in near]
+                    for row in range(rows):
+                        summed = None
+                        for a in range(3):
+                            if not 0 <= row + a - 1 < rows:
+                                continue
+                            for b in range(3):
+                                tap = taps[layer, 3 * a + b : 3 * a + b + 1, part_lanes]
+                                term = tap * cols[b][row + a - 1]
+                                summed = term if summed is None else summed + term
+                        conv[t, row * per_tile : (row + 1) * per_tile, part_lanes] = (
+                            summed.astype(BF16)
+                        )
+                return carry
+
+            lax.fori_loop(0, tiles, convolve_tile, 0)
+            step = 4 if tiles % 4 == 0 else 1
+
+            def mix_tiles(block, carry):
+                first = block * step
+                cells = conv[pl.ds(first, step)].reshape(step * rows * per_tile, channels)
+                mixed = jnp.dot(cells, weights[layer], preferred_element_type=F32)
+                for n in range(step):
+                    for row in range(rows):
+                        at = (n * rows + row) * per_tile
+                        factor = gain[layer, pl.ds((first + n) * lat + 2 * row + parity, 1), :]
+                        fields[parity, first + n, row] = (
+                            fields[parity, first + n, row].astype(F32)
+                            + factor * mixed[at : at + per_tile]
+                        ).astype(BF16)
+                return carry
+
+            lax.fori_loop(0, tiles // step, mix_tiles, 0)
+
+    own_out = [
+        pltpu.make_async_copy(
+            fields.at[parity, tile, :, :, lanes(chan)],
+            img.at[parity, chan, :, vectors(tile), :],
+            own_sem.at[1, parity],
+        )
+        for parity in range(2)
+    ]
+    for parity in range(2):
+        own_in[parity].wait()
+        each_step(lambda step: copy_in(parity, step, target(step), source(step)).wait_recv())
+        run_layers(parity)
+        own_out[parity].start()
+        each_step(lambda step: copy_out(parity, step, target(step), mine).start())
+
+    sketch_here.wait()
+    images_out = []
+    grams = jnp.zeros((2 * num_vectors, num_vectors), F32)
+    for parity in range(2):
+        own_out[parity].wait()
+        each_step(lambda step: copy_out(parity, step, target(step), source(step)).wait_recv())
+        for lon in range(2):
+            out = pltpu.make_async_copy(
+                img.at[parity, lon], img_hbm.at[:, parity, lon], local_sem.at[2 + 2 * parity + lon]
+            )
+            out.start()
+            images_out.append(out)
+        for row in range(rows):
+            here = jnp.concatenate([img[parity, 0, row], img[parity, 1, row]], axis=1)
+            start = jnp.concatenate([sketch[row, parity, 0], sketch[row, parity, 1]], axis=1)
+            grams = grams + lax.dot_general(
+                jnp.concatenate([here, start], axis=0), here, (((1,), (1,)), ((), ())),
+                preferred_element_type=F32,
+            )
+    acc[...] = grams
+    each_step(lambda step: copy_part(step, target(step)).start())
+    each_step(lambda step: copy_part(step, target(step)).wait_recv())
+    summed = acc[share_of(me), :]
+    for step in range(1, count):
+        summed = summed + part[step]
+    total[share_of(me), :] = summed * scale
+    each_step(lambda step: copy_total(step, target(step), mine).start())
+
+    copy_taps(mine).wait_send()
+    copy_weights(mine).wait_send()
+    each_step(lambda step: copy_base(step, target(step), mine).wait_send())
+    for parity in range(2):
+        each_step(lambda step: copy_in(parity, step, target(step), mine).wait_send())
+        each_step(lambda step: copy_out(parity, step, target(step), mine).wait_send())
+    each_step(lambda step: copy_part(step, target(step)).wait_send())
+    for out in images_out:
+        out.wait()
+    each_step(lambda step: copy_total(step, target(step), source(step)).wait_recv())
+    gram_ref[0] = total[:num_vectors]
+    gram_ref[1] = total[num_vectors:]
+    each_step(lambda step: copy_total(step, target(step), mine).wait_send())
+
+
+def per_device_transposed(sketch_vectors, base_state, depth_taps, mix_weight):
+    tiles, chans = lax.axis_size("tile"), lax.axis_size("chan")
+    count = tiles * chans
+    lat, lon, num_vectors, width = sketch_vectors.shape
+    rows = lat // 2
+    per_tile = num_vectors // tiles
+    channels = chans * width
+    scale = 1.0 / (lat * lon * tiles * channels)
+    split = sketch_vectors.reshape(rows, 2, lon, num_vectors, width)
+    images, gram = pl.pallas_call(
+        functools.partial(transposed_kernel, tiles, chans, scale),
+        out_shape=(
+            jax.ShapeDtypeStruct(split.shape, BF16),
+            jax.ShapeDtypeStruct((2, num_vectors, num_vectors), F32),
+        ),
+        in_specs=[
+            pl.BlockSpec(memory_space=pl.ANY),
+            pl.BlockSpec(memory_space=pltpu.VMEM),
+            pl.BlockSpec(memory_space=pltpu.VMEM),
+            pl.BlockSpec(memory_space=pl.ANY),
+        ],
+        out_specs=(pl.BlockSpec(memory_space=pl.ANY), pl.BlockSpec(memory_space=pltpu.VMEM)),
+        scratch_shapes=[
+            pltpu.VMEM((2, tiles, rows, per_tile, channels), BF16),
+            pltpu.VMEM(split.shape, BF16),
+            pltpu.VMEM((2, lon, rows, num_vectors, width), BF16),
+            pltpu.VMEM((LAYERS, channels, channels), BF16),
+            pltpu.VMEM((LAYERS, 16, channels), F32),
+            pltpu.VMEM((2 * lat, width), F32),
+            pltpu.VMEM((tiles, chans, 2 * lat, width), BF16),
+            pltpu.VMEM((tiles, rows * per_tile, channels), BF16),
+            pltpu.VMEM((LAYERS, tiles * lat, channels), F32),
+            pltpu.VMEM((2 * num_vectors, num_vectors), F32),
+            pltpu.VMEM((count, 2 * num_vectors // count, num_vectors), F32),
+            pltpu.VMEM((2 * num_vectors, num_vectors), F32),
+            pltpu.SemaphoreType.DMA((6,)),
+            pltpu.SemaphoreType.DMA((2, 2)),
+            pltpu.SemaphoreType.DMA((count,)),
+            pltpu.SemaphoreType.DMA((count,)),
+            pltpu.SemaphoreType.DMA((2,)),
+            pltpu.SemaphoreType.DMA((2,)),
+            pltpu.SemaphoreType.DMA((2, count)),
+            pltpu.SemaphoreType.DMA((2, count)),
+            pltpu.SemaphoreType.DMA((2, count)),
+            pltpu.SemaphoreType.DMA((2, count)),
+            pltpu.SemaphoreType.DMA((count,)),
+            pltpu.SemaphoreType.DMA((count,)),
+            pltpu.SemaphoreType.DMA((count,)),
+            pltpu.SemaphoreType.DMA((count,)),
+        ],
+        compiler_params=pltpu.CompilerParams(
+            collective_id=0, has_side_effects=True, vmem_limit_bytes=32 * 1024 * 1024
+        ),
+    )(split, base_state, depth_taps, mix_weight)
+    return images.reshape(sketch_vectors.shape), gram
+
+
+def fits_transposed(shape, mesh_shape):
+    lat, lon, num_vectors, width = shape
+    tiles, chans = mesh_shape["tile"], mesh_shape["chan"]
+    return (
+        lat == 8 and lon == 2 and chans == 2 and width % 128 == 0
+        and num_vectors == width == 128 and tiles > 1
+        and num_vectors % (16 * tiles) == 0 and (2 * num_vectors) % (8 * tiles * chans) == 0
+    )
+
+
+def local_step(mesh_shape, *args):
+    if fits_transposed(args[0].shape, mesh_shape):
+        return per_device_transposed(*args)
+    return per_device(*args)
+
+
 def solution(mesh):
     in_specs = (
         P(None, "tile", "grp", "chan"),
@@ -74,5 +424,5 @@
     )
     out_specs = (P(None, "tile", "grp", "chan"), P("grp", None, None))
     return jax.shard_map(
-        per_device, mesh=mesh, in_specs=in_specs, out_specs=out_specs, check_vma=False
+        functools.partial(local_step, dict(mesh.shape)), mesh=mesh, in_specs=in_specs, out_specs=out_specs, check_vma=False
     )

time: 235 us -> 49.5 us (0.21)
  waiting for transfers between devices: 182 us -> 0 us
  Pallas kernels: 0 us -> 44.5 us
  starting transfers between devices: 15.8 us -> 0 us
  other arithmetic: 14.8 us -> 0 us
  between operations: 14.1 us -> 0.65 us
  matrix products: 5.62 us -> 0 us
    psum x1 -> x0, waiting for transfers between devices: 88.6 us -> none  [per_device(): summed = lax.psum(jnp.stack([first, second]), ('tile', 'chan'))]
    ppermute x6 -> x0, waiting for transfers between devices: 65.9 us -> none  [the longest x3 59.6 us: extended_2(): lax.ppermute(lax.slice_in_dim(block, block.shape[dim] - width, None, axis...]
    pallas_call x0 -> x1, Pallas kernels: none -> 44.5 us  [per_device_transposed(): pl.pallas_call(functools.partial(transposed_kernel, tiles, chans, scale),...]
    all_gather x3 -> x0, waiting for transfers between devices: 27.3 us -> none  [per_device(): lax.all_gather(conv, 'chan', axis=3, tiled=True)]
    ppermute x6 -> x0, starting transfers between devices: 15.6 us -> none  [the longest x3 9.04 us: extended_2(): lax.ppermute(lax.slice_in_dim(block, 0, width, axis=dim), axis, backward)]
    concatenate x6 -> x0, other arithmetic: 6.33 us -> none  [the longest x3 4.83 us: extended_2(): block = jnp.concatenate([low, block, high], axis=dim)]
    dot_general x5 -> x0, matrix products: 5.62 us -> none  [the longest x3 5.04 us: per_device(): jnp.dot(lax.all_gather(conv, 'chan', axis=3, tiled=True), layer_mix, pref...]
    convert_element_type x5 -> x0, other arithmetic: 5.6 us -> none  [the longest x3 5.58 us: convolve(): return summed.astype(jnp.bfloat16)]
  transfers between devices with their start and end apart: 10 -> 0, of which waited for: 10 -> 0; matrix products, arithmetic and copies ran while one was open for 0% -> 0% of each run, Pallas kernels for 0% -> 0%
where the time goes in v1:
time: 49.5 us; the launch traced here: 49.3 us
  Pallas kernels  44.5 us (90%)
  local copies, waits for them, and re-layouts  4.13 us (8%)
  between operations  0.65 us (1%)
    pallas_call x1, Pallas kernels, per_device_transposed(): pl.pallas_call(functools.partial(transposed_kernel, tiles, chans, scale),...  44.5 us
    unnamed x9, local copies, waits for them, and re-layouts  4.13 us

profile of v1, /device:TPU:0, one launch (start us, length us, event | category | flops | bytes accessed | tf_op | source)
XLA Modules:
  0.0 49.3 jit_solution(16879601813892420876)
XLA Ops:
  0.6 0.0 copy-start.2
  0.6 0.7 %copy.6.taps_ref = bf16[3,9,128]{2,1,0:T(8,128)(2,1)S(1)} copy(bf16[3,9,128]{2,0,1:T(4,128)(2,1)} %param.6) | data formatting | bytes 13824 | tf_op args[2]
  1.3 0.0 copy-done.2
  1.4 0.0 copy-start
  1.4 1.0 %copy-done = bf16[8,2,128,128]{3,2,1,0:T(8,128)(2,1)S(1)} copy-done((bf16[8,2,128,128]{3,2,1,0:T(8,128)(2,1)S(1)}, bf16[8,2,128,128]{3,2,1,0:T(8,128)(2,1)}, u32[]{:S(2)}) %copy-start) | copy-done | bytes 524312
  2.4 0.0 copy-start.1
  2.4 0.9 %copy-done.1 = bf16[3,256,128]{2,1,0:T(8,128)(2,1)S(1)} copy-done((bf16[3,256,128]{2,1,0:T(8,128)(2,1)S(1)}, bf16[3,256,128]{2,1,0:T(8,128)(2,1)}, u32[]{:S(2)}) %copy-start.1) | copy-done | bytes 196632
  3.3 44.5 %shard_map.59 = (bf16[4,2,2,128,128]{4,3,2,1,0:T(8,128)(2,1)S(1)}, f32[2,128,128]{2,1,0:T(8,128)S(1)}) custom-call(bf16[4,2,2,128,128]{4,3,2,1,0:T(8,128)(2,1)S(1)} %bitcast.2, bf16[8,2,128]{2,1,0:T(2,128)(2,1)S(1)} %copy-done.2, bf16[3,9,128]{2,1,0:T(8,128)(2,1)S(1)} %copy.6.taps_ref, bf16[3,256,128]{2,1,0:T(8,128)(2,1)S(1)} %copy-done.1), custom_call_target="tpu_custom_call" | custom-call | tf_op jit(solution)/shard_map/pallas_call | solution.py:354
  47.8 0.8 %copy.9 = bf16[8,2,128,128]{3,2,1,0:T(8,128)(2,1)} copy(bf16[8,2,128,128]{3,2,1,0:T(8,128)(2,1)S(1)} %bitcast.3) | data formatting | bytes 1048576
  48.6 0.7 %copy.10 = f32[2,128,128]{2,1,0:T(8,128)} copy(f32[2,128,128]{2,1,0:T(8,128)S(1)} %get-tuple-element.9) | data formatting | bytes 262144
Async XLA Ops:
  0.6 0.7 %copy-start.2 = (bf16[8,2,128]{2,1,0:T(2,128)(2,1)S(1)}, bf16[8,2,128]{2,1,0:T(2,128)(2,1)}, u32[]{:S(2)}) copy-start(bf16[8,2,128]{2,1,0:T(2,128)(2,1)} %base_ref.1) | copy-start | bytes 12292
  1.4 1.0 %copy-start = (bf16[8,2,128,128]{3,2,1,0:T(8,128)(2,1)S(1)}, bf16[8,2,128,128]{3,2,1,0:T(8,128)(2,1)}, u32[]{:S(2)}) copy-start(bf16[8,2,128,128]{3,2,1,0:T(8,128)(2,1)} %param.4) | copy-start | bytes 1572868
  2.4 0.9 %copy-start.1 = (bf16[3,256,128]{2,1,0:T(8,128)(2,1)S(1)}, bf16[3,256,128]{2,1,0:T(8,128)(2,1)}, u32[]{:S(2)}) copy-start(bf16[3,256,128]{2,1,0:T(8,128)(2,1)} %mix_hbm.1) | copy-start | bytes 589828

commit v2 on v1

--- a/solution.py
+++ b/solution.py
@@ -74,7 +74,7 @@
 
 def transposed_kernel(
     tiles, chans, scale, sk_hbm, base_ref, taps_ref, mix_hbm, img_hbm, gram_ref,
-    fields, sketch, img, weights, taps, base_rows, base_all, conv, gain, acc, part, total,
+    fields, sketch, img, weights, taps, base_rows, base_all, conv, gain, acc, paired, part, total,
     local_sem, own_sem, base_send, base_recv, pair_send, pair_recv,
     in_send, in_recv, out_send, out_recv, red_send, red_recv, all_send, all_recv,
 ):
@@ -84,7 +84,7 @@
     rows, _, _, num_vectors, width = sk_hbm.shape
     per_tile = num_vectors // tiles
     channels = chans * width
-    share = 2 * num_vectors // count
+    share = num_vectors // tiles
 
     def device(index):
         return lax.div(index, chans), lax.rem(index, chans)
@@ -117,6 +117,16 @@
 
         lax.fori_loop(1, count, wrapped, 0)
 
+    def each_tile(body):
+        def wrapped(step, carry):
+            body(step)
+            return carry
+
+        lax.fori_loop(1, tiles, wrapped, 0)
+
+    def next_tile(step):
+        return lax.rem(tile + step, tiles), chan
+
     def copy_in(parity, step, to, of):
         return remote(
             sk_hbm.at[:, parity, to[1], vectors(to[0]), :],
@@ -139,13 +149,12 @@
 
     def copy_part(step, to):
         return remote(
-            acc.at[share_of(to[0] * chans + to[1])], part.at[step],
-            red_send.at[step], red_recv.at[step], to,
+            paired.at[0, share_of(to[0])], part.at[step], red_send.at[step], red_recv.at[step], to
         )
 
     def copy_total(step, to, of):
         return remote(
-            total.at[share_of(me)], total.at[share_of(of[0] * chans + of[1])],
+            total.at[chan, share_of(tile)], total.at[of[1], share_of(of[0])],
             all_send.at[step], all_recv.at[step], to,
         )
 
@@ -318,13 +327,20 @@
                 jnp.concatenate([here, start], axis=0), here, (((1,), (1,)), ((), ())),
                 preferred_element_type=F32,
             )
-    acc[...] = grams
-    each_step(lambda step: copy_part(step, target(step)).start())
-    each_step(lambda step: copy_part(step, target(step)).wait_recv())
-    summed = acc[share_of(me), :]
-    for step in range(1, count):
+    acc[0] = grams[:num_vectors]
+    acc[1] = grams[num_vectors:]
+    swap = remote(
+        acc.at[lax.rem(chan + 1, chans)], paired.at[1], pair_send.at[2], pair_recv.at[2], other
+    )
+    swap.start()
+    swap.wait_recv()
+    paired[0] = acc[chan] + paired[1]
+    each_tile(lambda step: copy_part(step, next_tile(step)).start())
+    each_tile(lambda step: copy_part(step, next_tile(step)).wait_recv())
+    summed = paired[0, share_of(tile), :]
+    for step in range(1, tiles):
         summed = summed + part[step]
-    total[share_of(me), :] = summed * scale
+    total[chan, share_of(tile), :] = summed * scale
     each_step(lambda step: copy_total(step, target(step), mine).start())
 
     copy_taps(mine).wait_send()
@@ -333,12 +349,12 @@
     for parity in range(2):
         each_step(lambda step: copy_in(parity, step, target(step), mine).wait_send())
         each_step(lambda step: copy_out(parity, step, target(step), mine).wait_send())
-    each_step(lambda step: copy_part(step, target(step)).wait_send())
+    swap.wait_send()
+    each_tile(lambda step: copy_part(step, next_tile(step)).wait_send())
     for out in images_out:
         out.wait()
     each_step(lambda step: copy_total(step, target(step), source(step)).wait_recv())
-    gram_ref[0] = total[:num_vectors]
-    gram_ref[1] = total[num_vectors:]
+    gram_ref[...] = total[...]
     each_step(lambda step: copy_total(step, target(step), mine).wait_send())
 
 
@@ -374,15 +390,16 @@
             pltpu.VMEM((tiles, chans, 2 * lat, width), BF16),
             pltpu.VMEM((tiles, rows * per_tile, channels), BF16),
             pltpu.VMEM((LAYERS, tiles * lat, channels), F32),
-            pltpu.VMEM((2 * num_vectors, num_vectors), F32),
-            pltpu.VMEM((count, 2 * num_vectors // count, num_vectors), F32),
-            pltpu.VMEM((2 * num_vectors, num_vectors), F32),
+            pltpu.VMEM((2, num_vectors, num_vectors), F32),
+            pltpu.VMEM((2, num_vectors, num_vectors), F32),
+            pltpu.VMEM((tiles, num_vectors // tiles, num_vectors), F32),
+            pltpu.VMEM((2, num_vectors, num_vectors), F32),
             pltpu.SemaphoreType.DMA((6,)),
             pltpu.SemaphoreType.DMA((2, 2)),
             pltpu.SemaphoreType.DMA((count,)),
             pltpu.SemaphoreType.DMA((count,)),
-            pltpu.SemaphoreType.DMA((2,)),
-            pltpu.SemaphoreType.DMA((2,)),
+            pltpu.SemaphoreType.DMA((3,)),
+            pltpu.SemaphoreType.DMA((3,)),
             pltpu.SemaphoreType.DMA((2, count)),
             pltpu.SemaphoreType.DMA((2, count)),
             pltpu.SemaphoreType.DMA((2, count)),
@@ -405,7 +422,7 @@
     return (
         lat == 8 and lon == 2 and chans == 2 and width % 128 == 0
         and num_vectors == width == 128 and tiles > 1
-        and num_vectors % (16 * tiles) == 0 and (2 * num_vectors) % (8 * tiles * chans) == 0
+        and num_vectors % (16 * tiles) == 0 and lon == chans
     )
 
 

time: 49.5 us -> 49.7 us (level)
  no operation moved by 1% of the time
where the time goes in v2:
time: 49.7 us; the launch traced here: 49.4 us
  Pallas kernels  44.6 us (90%)
  local copies, waits for them, and re-layouts  4.13 us (8%)
  between operations  0.65 us (1%)
    pallas_call x1, Pallas kernels, per_device_transposed(): pl.pallas_call(functools.partial(transposed_kernel, tiles, chans, scale),...  44.6 us
    unnamed x9, local copies, waits for them, and re-layouts  4.13 us

profile of v2, /device:TPU:0, one launch (start us, length us, event | category | flops | bytes accessed | tf_op | source)
XLA Modules:
  0.0 49.4 jit_solution(15170551032973352827)
XLA Ops:
  0.6 0.0 copy-start.2
  0.6 0.7 %copy.6.taps_ref = bf16[3,9,128]{2,1,0:T(8,128)(2,1)S(1)} copy(bf16[3,9,128]{2,0,1:T(4,128)(2,1)} %param.6) | data formatting | bytes 13824 | tf_op args[2]
  1.3 0.0 copy-done.2
  1.4 0.0 copy-start
  1.4 1.0 %copy-done = bf16[8,2,128,128]{3,2,1,0:T(8,128)(2,1)S(1)} copy-done((bf16[8,2,128,128]{3,2,1,0:T(8,128)(2,1)S(1)}, bf16[8,2,128,128]{3,2,1,0:T(8,128)(2,1)}, u32[]{:S(2)}) %copy-start) | copy-done | bytes 524312
  2.4 0.0 copy-start.1
  2.4 0.9 %copy-done.1 = bf16[3,256,128]{2,1,0:T(8,128)(2,1)S(1)} copy-done((bf16[3,256,128]{2,1,0:T(8,128)(2,1)S(1)}, bf16[3,256,128]{2,1,0:T(8,128)(2,1)}, u32[]{:S(2)}) %copy-start.1) | copy-done | bytes 196632
  3.3 44.6 %shard_map.59 = (bf16[4,2,2,128,128]{4,3,2,1,0:T(8,128)(2,1)S(1)}, f32[2,128,128]{2,1,0:T(8,128)S(1)}) custom-call(bf16[4,2,2,128,128]{4,3,2,1,0:T(8,128)(2,1)S(1)} %bitcast.2, bf16[8,2,128]{2,1,0:T(2,128)(2,1)S(1)} %copy-done.2, bf16[3,9,128]{2,1,0:T(8,128)(2,1)S(1)} %copy.6.taps_ref, bf16[3,256,128]{2,1,0:T(8,128)(2,1)S(1)} %copy-done.1), custom_call_target="tpu_custom_call" | custom-call | tf_op jit(solution)/shard_map/pallas_call | solution.py:370
  48.0 0.8 %copy.9 = bf16[8,2,128,128]{3,2,1,0:T(8,128)(2,1)} copy(bf16[8,2,128,128]{3,2,1,0:T(8,128)(2,1)S(1)} %bitcast.3) | data formatting | bytes 1048576
  48.7 0.7 %copy.10 = f32[2,128,128]{2,1,0:T(8,128)} copy(f32[2,128,128]{2,1,0:T(8,128)S(1)} %get-tuple-element.9) | data formatting | bytes 262144
Async XLA Ops:
  0.6 0.7 %copy-start.2 = (bf16[8,2,128]{2,1,0:T(2,128)(2,1)S(1)}, bf16[8,2,128]{2,1,0:T(2,128)(2,1)}, u32[]{:S(2)}) copy-start(bf16[8,2,128]{2,1,0:T(2,128)(2,1)} %base_ref.1) | copy-start | bytes 12292
  1.4 1.0 %copy-start = (bf16[8,2,128,128]{3,2,1,0:T(8,128)(2,1)S(1)}, bf16[8,2,128,128]{3,2,1,0:T(8,128)(2,1)}, u32[]{:S(2)}) copy-start(bf16[8,2,128,128]{3,2,1,0:T(8,128)(2,1)} %param.4) | copy-start | bytes 1572868
  2.4 0.9 %copy-start.1 = (bf16[3,256,128]{2,1,0:T(8,128)(2,1)S(1)}, bf16[3,256,128]{2,1,0:T(8,128)(2,1)}, u32[]{:S(2)}) copy-start(bf16[3,256,128]{2,1,0:T(8,128)(2,1)} %mix_hbm.1) | copy-start | bytes 589828
